TPU v7x, 32 devices: a whole 2x2x4 slice. The times are simulated.
32 devices in a mesh: parts: 2 (over y), frag: 8 (over z, x), orb: 2 (over core).
Axes of the slice: x: 2, y: 2, z: 4, core: 2. Of those that a mesh axis runs over, the one named last changes fastest.
Arguments:
- potential: float32 [128, 768], P(('parts', 'frag')), parts along dimension 0, may hold values from -1 to 1
- orbitals: bfloat16 [16, 128, 4096], P(('parts', 'frag'), None, 'orb'), parts along dimension 0, may hold values from -6 to 6
- offsets: int32 [16, 3], P('parts'), parts along dimension 0, may hold values from 0 to 56, as said below
- weight_signs: int32 [16], P('parts'), parts along dimension 0, may hold values from -1 to 1, as said below
- assignment: int32 [16], P('parts'), parts along dimension 0, may hold values from 0 to 7, each once
Outputs:
- density: float32 [128, 768], P(('parts', 'frag')), parts along dimension 0
- orbitals_out: float32 [16, 128, 4096], P(('parts', 'frag'), None, 'orb'), parts along dimension 0
There are 2 independent parts, one for each index of `parts`. A program takes and returns all parts, laid end to end along the dimension named above; each array names one. Nothing has to cross between parts.
Inputs may be any that keep to these rules, and one draw needn't show every extreme that they name: offsets[f] = (oz, ox, oy): oz is 8 times a slab number below 8, ox is 0 or 8, oy is 0, 8 or 16; some fragment lies on the last slab with corner (8, 16) in x and y, and some fragment has ox = 0. `weight_signs`: each entry is -1 or 1.
All inputs are finite; a program needn't handle non-finite values.
Results may differ from a plain program's by a relative error of at most 0.0003.
Values sent between devices are 32-bit elements; how exact they have to be, the bound alone decides.
A program may use at most 64 MiB of HBM per device.

v0:
```python
import jax
import jax.numpy as jnp
from jax import lax
from jax.sharding import PartitionSpec as P

NORB = 128
FSIDE = 16
DEGREE = 8
PASSES = 3
SLAB = 8
PLANE = 256
FCELLS = 4096
GX = 24
GY = 32


SPECTRUM_MID = 3.5
SPECTRUM_HALF = 3.75
OCCUPY_SLOPE = 0.2


def extended(shard, sides, width):
    for axis, dim in sides:
        size, length = (lax.axis_size(axis), shard.shape[dim])
        up = [(i, (i + 1) % size) for i in range(size - 1)]
        down = [(j, i) for i, j in up]
        last = lax.slice_in_dim(shard, length - width, length, axis=dim)
        first = lax.slice_in_dim(shard, 0, width, axis=dim)
        before = lax.ppermute(last, axis, up)
        after = lax.ppermute(first, axis, down)
        shard = jnp.concatenate([before, shard, after], axis=dim)
    return shard


def plane_sum(states, side_len):
    plane_len = states.shape[-1]
    pads = [(0, 0)] * (states.ndim - 1) + [(side_len, side_len)]
    padded = jnp.pad(states, pads)
    summed = padded[..., 2 * side_len :] + padded[..., :plane_len]
    column = lax.broadcasted_iota(jnp.int32, (plane_len,), 0) % side_len
    y_after = padded[..., side_len + 1 : side_len + 1 + plane_len]
    y_before = padded[..., side_len - 1 : side_len - 1 + plane_len]
    zero_val = jnp.zeros_like(y_after)
    return (
        summed
        + jnp.where(column < side_len - 1, y_after, zero_val)
        + jnp.where(column > 0, y_before, zero_val)
    )


def hamiltonian(padded, local_potential, side_len):
    centre = padded[:, 1:-1]
    neighbours = padded[:, 2:] + padded[:, :-2] + plane_sum(centre, side_len)
    return (3.0 + local_potential) * centre - 0.5 * neighbours


def chebyshev(states, operate):
    previous = states
    current = (operate(states) - SPECTRUM_MID * states) / SPECTRUM_HALF
    for repeat in range(DEGREE - 1):
        following = 2.0 * (operate(current) - SPECTRUM_MID * current) / SPECTRUM_HALF - previous
        previous, current = (current, following)
    return current


def gram(left, right):
    rows_left = left.reshape(left.shape[0], -1)
    rows_right = right.reshape(right.shape[0], -1)
    product = jnp.dot(
        rows_left, rows_right.T, precision=lax.Precision.HIGHEST, preferred_element_type=jnp.float32
    )
    return product / FCELLS


def orthonormal(matrix, states):
    lower = jnp.linalg.cholesky(matrix)
    flat = states.reshape(states.shape[0], -1)
    solved = lax.linalg.triangular_solve(lower, flat, left_side=True, lower=True)
    return (solved.reshape(states.shape), lower)


def occupation(projected):
    order_len = projected.shape[0]
    eye_mat = jnp.eye(order_len, dtype=jnp.float32)
    shifted = projected - jnp.trace(projected) / order_len * eye_mat
    occupied = 0.5 * eye_mat - OCCUPY_SLOPE * shifted
    for repeat in range(2):
        square = jnp.dot(
            occupied, occupied, precision=lax.Precision.HIGHEST, preferred_element_type=jnp.float32
        )
        cube = jnp.dot(
            square, occupied, precision=lax.Precision.HIGHEST, preferred_element_type=jnp.float32
        )
        occupied = 3.0 * square - 2.0 * cube
    return occupied


def fragment_density(states, occupied, sign_val):
    flat = states.reshape(states.shape[0], -1)
    mixed = jnp.dot(
        occupied, flat, precision=lax.Precision.HIGHEST, preferred_element_type=jnp.float32
    )
    return sign_val * jnp.sum(flat * mixed, axis=0) / NORB


def local(potential, orbitals, offsets, weight_signs, assignment):
    frag_count = lax.axis_size("frag")
    slot_index = lax.axis_index("frag")
    orb_index = lax.axis_index("orb")
    fragment = assignment[slot_index]
    place = offsets[fragment]
    zero_idx = place[0] * 0
    my_slab = (place[0] // SLAB + orb_index) % frag_count
    sign_val = weight_signs[fragment].astype(jnp.float32)
    row_len = potential.shape[1]
    piece = lax.all_gather(potential, "frag", axis=0, tiled=True)
    row_ids = lax.broadcasted_iota(jnp.int32, (piece.shape[0],), 0)
    wanted = my_slab * SLAB + lax.broadcasted_iota(jnp.int32, (SLAB,), 0)
    pick = (wanted[:, None] == row_ids[None, :]).astype(jnp.float32)
    mine_rows = jnp.dot(
        pick, piece, precision=lax.Precision.HIGHEST, preferred_element_type=jnp.float32
    )
    local_potential = lax.dynamic_slice(
        mine_rows.reshape(SLAB, GX, GY), (zero_idx, place[1], place[2]), (SLAB, FSIDE, FSIDE)
    ).reshape(SLAB, PLANE)
    states = orbitals[0].astype(jnp.float32).reshape(NORB, SLAB, PLANE)

    def operate(field_now):
        padded = extended(field_now, (("orb", 1),), 1)
        return hamiltonian(padded, local_potential, FSIDE)

    def filter_block(field_now):
        return chebyshev(field_now, operate)

    def summed_gram(left, right):
        return lax.psum(gram(left, right), "orb")

    for repeat in range(PASSES - 1):
        filtered = filter_block(states)
        states, lower = orthonormal(summed_gram(filtered, filtered), filtered)
    filtered = filter_block(states)
    states, lower = orthonormal(summed_gram(filtered, filtered), filtered)
    coupling = summed_gram(states, operate(states))
    projected = 0.5 * (coupling + coupling.T)
    occupied = occupation(projected)
    density_mine = fragment_density(states, occupied, sign_val).reshape(SLAB, PLANE)
    placed = lax.dynamic_update_slice(
        jnp.zeros((SLAB, GX, GY), jnp.float32),
        density_mine.reshape(SLAB, FSIDE, FSIDE),
        (zero_idx, place[1], place[2]),
    )
    placed = placed.reshape(SLAB, row_len)
    row_ids = lax.broadcasted_iota(jnp.int32, (SLAB * lax.axis_size("frag"),), 0)
    wanted = my_slab * SLAB + lax.broadcasted_iota(jnp.int32, (SLAB,), 0)
    pick = (row_ids[:, None] == wanted[None, :]).astype(jnp.float32)
    half_density = lax.psum_scatter(
        jnp.dot(pick, placed, precision=lax.Precision.HIGHEST, preferred_element_type=jnp.float32),
        "frag",
        scatter_dimension=0,
        tiled=True,
    )
    density = lax.psum(half_density, "orb")
    return (density, states.reshape(1, NORB, SLAB * PLANE))


def solution(mesh):
    return jax.shard_map(
        local,
        mesh=mesh,
        in_specs=(
            P(("parts", "frag"), None),
            P(("parts", "frag"), None, "orb"),
            P("parts", None),
            P("parts"),
            P("parts"),
        ),
        out_specs=(P(("parts", "frag"), None), P(("parts", "frag"), None, "orb")),
        check_vma=False,
    )
```

profile of v0, /device:TPU:0, one launch (start us, length us, event | category | flops | bytes accessed | tf_op | source)
XLA Modules:
  0.0 454.9 jit_solution(12528182072153363277)
XLA Ops:
  9.8 3.0 collective-permute-start.1
  18.7 32.4 %all_gather.3 = f32[64,768]{1,0:T(8,128)S(1)} all-gather(f32[8,768]{1,0:T(8,128)S(1)} %copy-done.2), channel_id=1, replica_groups=mesh['parts'=2,'frag'=8,'orb'=2] {'frag'}, dimensions={0}, use_global_device_ids=true | all-gather | bytes 221184 | tf_op jit(solution)/shard_map/all_gather | solution.py:116
  57.8 3.0 collective-permute-start.3
  64.1 3.0 collective-permute-start.5
  70.5 3.0 collective-permute-start.7
  76.8 3.0 collective-permute-start.9
  83.1 3.0 collective-permute-start.11
  89.4 3.0 collective-permute-start.13
  95.6 3.0 collective-permute-start.15
  103.4 18.6 %all-reduce.30.cloned.1.call-done = f32[128,128]{0,1:T(8,128)} async-done(((f32[128,128]{0,1:T(8,128)}), f32[128,128]{0,1:T(8,128)}) %all-reduce.30.cloned.1.call-update) | async-done | bytes 65552 | tf_op jit(solution)/shard_map/psum | solution.py:136
  123.7 11.7 %cholesky.59 = f32[128,128]{1,0:T(8,128)S(1)} custom-call(f32[128,128]{1,0:T(8,128)S(1)} %fusion.309), custom_call_target="Cholesky" | custom-call | tf_op jit(solution)/shard_map/jit(cholesky)/cholesky | solution.py:76
  136.8 9.8 %custom-call.7 = f32[1,128,128]{1,2,0:T(8,128)S(1)} custom-call(f32[1,128,128]{2,1,0:T(8,128)S(1)} %fusion.297), custom_call_target="InvertDiagBlocksLowerTriangular" | custom-call | tf_op jit(solution)/shard_map/triangular_solve/custom-call.0 | solution.py:78
  161.5 3.0 collective-permute-start.21
  167.9 3.0 collective-permute-start.23
  174.2 3.0 collective-permute-start.25
  180.5 3.0 collective-permute-start.27
  186.8 3.0 collective-permute-start.29
  193.0 3.4 collective-permute-start.31
  200.6 19.0 %all-reduce.32.cloned.1.call-done = f32[128,128]{0,1:T(8,128)} async-done(((f32[128,128]{0,1:T(8,128)}), f32[128,128]{0,1:T(8,128)}) %all-reduce.32.cloned.1.call-update) | async-done | bytes 65552 | tf_op jit(solution)/shard_map/psum | solution.py:136
  221.4 11.7 %cholesky.70 = f32[128,128]{1,0:T(8,128)S(1)} custom-call(f32[128,128]{1,0:T(8,128)S(1)} %fusion.306), custom_call_target="Cholesky" | custom-call | tf_op jit(solution)/shard_map/jit(cholesky)/cholesky | solution.py:76
  234.5 9.8 %custom-call.8 = f32[1,128,128]{1,2,0:T(8,128)S(1)} custom-call(f32[1,128,128]{2,1,0:T(8,128)S(1)} %fusion.298), custom_call_target="InvertDiagBlocksLowerTriangular" | custom-call | tf_op jit(solution)/shard_map/triangular_solve/custom-call.0 | solution.py:78
  259.2 3.0 collective-permute-start.37
  265.6 3.2 collective-permute-start.39
  284.5 3.0 collective-permute-start.45
  290.8 3.0 collective-permute-start.47
  298.3 19.0 %all-reduce.34.cloned.1.call-done = f32[128,128]{0,1:T(8,128)} async-done(((f32[128,128]{0,1:T(8,128)}), f32[128,128]{0,1:T(8,128)}) %all-reduce.34.cloned.1.call-update) | async-done | bytes 65552 | tf_op jit(solution)/shard_map/psum | solution.py:136
  319.1 11.7 %cholesky.81 = f32[128,128]{1,0:T(8,128)S(1)} custom-call(f32[128,128]{1,0:T(8,128)S(1)} %fusion.303), custom_call_target="Cholesky" | custom-call | tf_op jit(solution)/shard_map/jit(cholesky)/cholesky | solution.py:76
  332.1 9.8 %custom-call.9 = f32[1,128,128]{1,2,0:T(8,128)S(1)} custom-call(f32[1,128,128]{2,1,0:T(8,128)S(1)} %fusion.299), custom_call_target="InvertDiagBlocksLowerTriangular" | custom-call | tf_op jit(solution)/shard_map/triangular_solve/custom-call.0 | solution.py:78
  344.7 3.0 collective-permute-start.49
  353.5 17.6 %all-reduce.36.cloned.1.call-done = f32[128,128]{0,1:T(8,128)} async-done(((f32[128,128]{0,1:T(8,128)}), f32[128,128]{0,1:T(8,128)}) %all-reduce.36.cloned.1.call-update) | async-done | bytes 65552 | tf_op jit(solution)/shard_map/psum | solution.py:136
  382.0 61.5 %reduce-scatter.2.cloned.1.call-done = f32[8,768]{1,0:T(8,128)} async-done(((f32[64,768]{1,0:T(8,128)}), f32[8,768]{1,0:T(8,128)}) %reduce-scatter.2.cloned.1.call-update) | async-done | bytes 24592 | tf_op jit(solution)/shard_map/reduce_scatter | solution.py:156
  443.6 4.6 %psum.39 = f32[8,768]{1,0:T(8,128)} all-reduce(f32[8,768]{1,0:T(8,128)} %reduce-scatter.2.cloned.1.call-done), channel_id=1, replica_groups=mesh['parts'=2,'frag'=8,'orb'=2] {'orb'}, use_global_device_ids=true, to_apply=%region_9.12 | all-reduce | flops 6144 | bytes 49152 | tf_op jit(solution)/shard_map/psum | solution.py:162
  (199 shorter events, 134.3 us)
Async XLA Ops:
  7.2 114.7 %all-reduce.30.cloned.1.call-start = ((), (), s32[]{:S(2)}) async-start(), calls=%async_computation.1 | async-start | bytes 131072 | tf_op jit(solution)/shard_map/psum | solution.py:136
  8.5 47.0 %collective-permute-start = (f32[128,1,256]{0,2,1:T(8,128)S(1)}, f32[128,1,256]{0,2,1:T(8,128)S(1)}, u32[]{:S(2)}, u32[]{:S(2)}) collective-permute-start(f32[128,1,256]{0,2,1:T(8,128)S(1)} %get-tuple-element.58), channel_id=1, source_target_pairs={{1,0},{3,2},{5,4},{7,6},{9,8},{11,10},{13,12},{15,14},{17,16},{19,... | collective-permute-start | bytes 393224 | tf_op jit(solution)/shard_map/ppermute | solution.py:30
  9.8 45.7 %collective-permute-start.1 = (f32[128,1,256]{0,2,1:T(8,128)S(1)}, f32[128,1,256]{0,2,1:T(8,128)S(1)}, u32[]{:S(2)}, u32[]{:S(2)}) collective-permute-start(f32[128,1,256]{0,2,1:T(8,128)S(1)} %get-tuple-element.59), channel_id=1, source_target_pairs={{0,1},{2,3},{4,5},{6,7},{8,9},{10,11},{12,13},{14,15},{16,17},{18,... | collective-permute-start | bytes 393224 | tf_op jit(solution)/shard_map/ppermute | solution.py:29
  56.5 4.4 collective-permute-start.2
  57.8 4.0 collective-permute-start.3
  62.8 4.4 collective-permute-start.4
  69.2 4.4 collective-permute-start.6
  75.5 4.4 collective-permute-start.8
  81.8 4.4 collective-permute-start.10
  88.1 4.4 collective-permute-start.12
  94.3 4.4 collective-permute-start.14
  103.1 116.5 %all-reduce.32.cloned.1.call-start = ((), (), s32[]{:S(2)}) async-start(), calls=%async_computation.2 | async-start | bytes 131072 | tf_op jit(solution)/shard_map/psum | solution.py:136
  147.6 4.4 collective-permute-start.16
  153.9 4.4 collective-permute-start.18
  160.2 4.4 collective-permute-start.20
  166.6 4.4 collective-permute-start.22
  172.9 4.4 collective-permute-start.24
  179.2 4.4 collective-permute-start.26
  185.5 4.4 collective-permute-start.28
  191.7 4.8 %collective-permute-start.30 = (f32[128,1,256]{0,2,1:T(8,128)S(1)}, f32[128,1,256]{0,2,1:T(8,128)S(1)}, u32[]{:S(2)}, u32[]{:S(2)}) collective-permute-start(f32[128,1,256]{0,2,1:T(8,128)S(1)} %get-tuple-element.28), channel_id=1, source_target_pairs={{1,0},{3,2},{5,4},{7,6},{9,8},{11,10},{13,12},{15,14},{17,16},{19,... | collective-permute-start | bytes 393224 | tf_op jit(solution)/shard_map/ppermute | solution.py:30
  200.5 116.8 %all-reduce.34.cloned.1.call-start = ((), (), s32[]{:S(2)}) async-start(), calls=%async_computation.3 | async-start | bytes 131072 | tf_op jit(solution)/shard_map/psum | solution.py:136
  245.3 4.4 collective-permute-start.32
  251.5 4.4 collective-permute-start.34
  257.9 4.4 collective-permute-start.36
  264.3 4.5 collective-permute-start.38
  270.6 4.4 collective-permute-start.40
  276.9 4.4 collective-permute-start.42
  283.2 4.4 collective-permute-start.44
  289.4 4.4 collective-permute-start.46
  298.2 72.9 %all-reduce.36.cloned.1.call-start = ((), (), s32[]{:S(2)}) async-start(), calls=%async_computation.4 | async-start | bytes 131072 | tf_op jit(solution)/shard_map/psum | solution.py:136
  343.4 4.4 collective-permute-start.48
  352.0 91.6 %reduce-scatter.2.cloned.1.call-start = ((), (), s32[]{:S(2)}) async-start(), calls=%async_computation.5 | async-start | bytes 221184 | tf_op jit(solution)/shard_map/reduce_scatter | solution.py:156
  (28 other events, 154.3 us)
Sparse Core Ops, SparseCore 0:
  103.3 18.6 all-reduce.29
  200.7 18.9 all-reduce.31
  298.4 18.9 all-reduce.33
  352.1 18.9 all-reduce.35
  382.2 61.3 reduce-scatter.1
where the time goes:
time: 463 us; the launch traced here: 455 us
  waiting for transfers between devices  158 us (34%)
  starting transfers between devices  109 us (24%)
  other arithmetic  96.5 us (21%)
  blocking collectives  37 us (8%)
  between operations  25 us (5%)
  matrix products  17.9 us (4%)
  local copies, waits for them, and re-layouts  10.8 us (2%)
    ppermute x25, starting transfers between devices, extended(): before = lax.ppermute(last, axis, up)  76.6 us
    psum x4, waiting for transfers between devices, summed_gram(): return lax.psum(gram(left, right), 'orb')  74.2 us
    reduce_scatter x1, waiting for transfers between devices, local(): lax.psum_scatter(jnp.dot(pick, placed, precision=lax.Precision.HIGHEST, p...  61.5 us
    another operation x9, other arithmetic, orthonormal(): lower = jnp.linalg.cholesky(matrix)  37.2 us
    all_gather x1, blocking collectives, local(): piece = lax.all_gather(potential, 'frag', axis=0, tiled=True)  32.4 us
    ppermute x25, starting transfers between devices, extended(): after = lax.ppermute(first, axis, down)  32.3 us
    another operation x6, other arithmetic, orthonormal(): lax.linalg.triangular_solve(lower, flat, left_side=True, lower=True)  31.4 us
    ppermute x25, waiting for transfers between devices, extended(): before = lax.ppermute(last, axis, up)  22.2 us
  transfers between devices with their start and end apart: 55, of which 29 were waited for; matrix products, arithmetic and copies ran while one was open for 1% of the time, Pallas kernels for 0%

commit v1 on v0

v1 whole, which is shorter than its diff:
```python
import jax
import jax.numpy as jnp
from jax import lax
from jax.experimental import pallas as pl
from jax.experimental.pallas import tpu as pltpu
from jax.sharding import PartitionSpec as P

NORB = 128
FSIDE = 16
DEGREE = 8
PASSES = 3
SLAB = 8
PLANE = 256
FCELLS = 4096
GX = 24
GY = 32
PAD = FSIDE + 2
ROWS = 32
LOW = 8

SPECTRUM_MID = 3.5
SPECTRUM_HALF = 3.75
OCCUPY_SLOPE = 0.2
COUPLE = 1.0 / SPECTRUM_HALF
HIGHEST = lax.Precision.HIGHEST


def dot(left, right, dims):
    return lax.dot_general(
        left, right, (dims, ((), ())), precision=HIGHEST, preferred_element_type=jnp.float32
    )


def inverse_factor(matrix):
    panels = NORB // 8
    lane = lax.broadcasted_iota(jnp.int32, (8, NORB), 1)
    sub = lax.broadcasted_iota(jnp.int32, (8, NORB), 0)
    a = [matrix[8 * i : 8 * i + 8] for i in range(panels)]
    w = [jnp.where(lane == sub + 8 * i, 1.0, 0.0).astype(jnp.float32) for i in range(panels)]
    out = []

    def row(x, j):
        return jnp.broadcast_to(x[j : j + 1], (8, NORB))

    for k in range(panels):
        cols = {
            i: [jnp.broadcast_to(a[i][:, 8 * k + j : 8 * k + j + 1], (8, NORB)) for j in range(8)]
            for i in range(k, panels)
        }
        scale = jnp.zeros((8, NORB), jnp.float32)
        for j in range(8):
            root = lax.rsqrt(row(cols[k][j], j))
            inv = root * root
            scale = jnp.where(sub == j, root, scale)
            col_rows = [row(cols[k][l], j) * inv for l in range(j + 1, 8)]
            a_row = row(a[k], j) * inv
            w_row = row(w[k], j) * inv
            for i in range(k, panels):
                f = cols[i][j]
                if i == k:
                    f = jnp.where(sub > j, f, 0.0)
                for l in range(j + 1, 8):
                    cols[i][l] = cols[i][l] - f * col_rows[l - j - 1]
                a[i] = a[i] - f * a_row
                w[i] = w[i] - f * w_row
        out.append(w[k] * scale)
    return jnp.concatenate(out, axis=0)


def fragment_kernel(orb_ref, own_ref, other_ref, v_ref, states_ref, rho_ref, xa, xb, w_ref):
    orb = orb_ref[0]

    def clear(z, _):
        xa[z] = jnp.zeros((PAD, ROWS, NORB), jnp.float32)
        xb[z] = jnp.zeros((PAD, ROWS, NORB), jnp.float32)
        return 0

    lax.fori_loop(0, PAD, clear, 0)

    for z in range(SLAB):
        block = own_ref[:, PLANE * z : PLANE * (z + 1)].astype(jnp.float32).T
        xa[orb * SLAB + z + 1, 1 : FSIDE + 1, LOW : LOW + FSIDE, :] = block.reshape(FSIDE, FSIDE, NORB)
        block = other_ref[:, PLANE * z : PLANE * (z + 1)].T
        xa[(1 - orb) * SLAB + z + 1, 1 : FSIDE + 1, LOW : LOW + FSIDE, :] = block.reshape(FSIDE, FSIDE, NORB)

    mid = pl.ds(LOW, FSIDE)

    def stencil(src, z, x):
        c = src[z + 1, x + 1, mid, :]
        n = src[z, x + 1, mid, :] + src[z + 2, x + 1, mid, :]
        n = n + (src[z + 1, x, mid, :] + src[z + 1, x + 2, mid, :])
        n = n + (src[z + 1, x + 1, pl.ds(LOW - 1, FSIDE), :] + src[z + 1, x + 1, pl.ds(LOW + 1, FSIDE), :])
        return v_ref[z, x] * c - COUPLE * n

    def first(src, dst):
        def body(z, _):
            for x in range(FSIDE):
                dst[z + 1, x + 1, mid, :] = 0.5 * stencil(src, z, x)
            return 0

        lax.fori_loop(0, FSIDE, body, 0)

    def later(src, dst):
        def body(z, _):
            for x in range(FSIDE):
                dst[z + 1, x + 1, mid, :] = stencil(src, z, x) - dst[z + 1, x + 1, mid, :]
            return 0

        lax.fori_loop(0, FSIDE, body, 0)

    def plane(src, z):
        return src[z + 1, 1 : FSIDE + 1, mid, :].reshape(PLANE, NORB)

    def one_pass(_, carry):
        first(xa, xb)
        later(xb, xa)

        def pair(_, c):
            later(xa, xb)
            later(xb, xa)
            return c

        lax.fori_loop(0, DEGREE // 2 - 1, pair, 0)

        def add(z, total):
            y = plane(xa, z)
            return total + dot(y, y, ((0,), (0,)))

        total = lax.fori_loop(0, FSIDE, add, jnp.zeros((NORB, NORB), jnp.float32))
        w_ref[...] = inverse_factor(total / FCELLS)

        def apply(z, c):
            s = dot(plane(xa, z), w_ref[...], ((1,), (1,)))
            xa[z + 1, 1 : FSIDE + 1, mid, :] = s.reshape(FSIDE, FSIDE, NORB)
            return c

        lax.fori_loop(0, FSIDE, apply, 0)
        return carry

    lax.fori_loop(0, PASSES, one_pass, 0)

    def couple(z, total):
        parts = []
        for x in range(FSIDE):
            parts.append((SPECTRUM_HALF / 2) * stencil(xa, z, x) + SPECTRUM_MID * xa[z + 1, x + 1, mid, :])
        h = jnp.concatenate(parts, axis=0)
        return total + dot(plane(xa, z), h, ((0,), (0,)))

    coupling = lax.fori_loop(0, FSIDE, couple, jnp.zeros((NORB, NORB), jnp.float32)) / FCELLS
    projected = 0.5 * (coupling + coupling.T)
    rows = lax.broadcasted_iota(jnp.int32, (NORB, NORB), 0)
    columns = lax.broadcasted_iota(jnp.int32, (NORB, NORB), 1)
    eye = jnp.where(rows == columns, 1.0, 0.0).astype(jnp.float32)
    trace = jnp.sum(projected * eye)
    occupied = 0.5 * eye - OCCUPY_SLOPE * (projected - trace / NORB * eye)
    for _ in range(2):
        square = dot(occupied, occupied, ((1,), (0,)))
        cube = dot(square, occupied, ((1,), (0,)))
        occupied = 3.0 * square - 2.0 * cube
    w_ref[...] = occupied
    ones = jnp.ones((8, NORB), jnp.float32)

    def density(z, c):
        s = plane(xa, z)
        m = s * dot(s, w_ref[...], ((1,), (0,)))
        r = dot(ones, m, ((1,), (1,)))
        rho_ref[pl.ds(z, 1), :] = r[0:1]
        return c

    lax.fori_loop(0, FSIDE, density, 0)
    for z in range(SLAB):
        states_ref[:, PLANE * z : PLANE * (z + 1)] = plane(xa, orb * SLAB + z).T


def local(potential, orbitals, offsets, weight_signs, assignment):
    frag_count = lax.axis_size("frag")
    slot_index = lax.axis_index("frag")
    orb_index = lax.axis_index("orb")
    own = orbitals[0]
    other = lax.ppermute(own.astype(jnp.float32), "orb", [(0, 1), (1, 0)])
    place = offsets[assignment[slot_index]]
    zero_idx = place[0] * 0
    piece = lax.all_gather(potential, "frag", axis=0, tiled=True)
    piece = jnp.concatenate([piece, piece[:SLAB]], axis=0).reshape(-1, GX, GY)
    v = lax.dynamic_slice(piece, (place[0], place[1], place[2]), (FSIDE, FSIDE, FSIDE))
    v = (v + (3.0 - SPECTRUM_MID)) * (2.0 / SPECTRUM_HALF)
    v = jnp.broadcast_to(v[..., None], (FSIDE, FSIDE, FSIDE, NORB))
    vmem = pl.BlockSpec(memory_space=pltpu.VMEM)
    states, rho = pl.pallas_call(
        fragment_kernel,
        out_shape=(
            jax.ShapeDtypeStruct((NORB, SLAB * PLANE), jnp.float32),
            jax.ShapeDtypeStruct((FSIDE, PLANE), jnp.float32),
        ),
        in_specs=[pl.BlockSpec(memory_space=pltpu.SMEM), vmem, vmem, vmem],
        out_specs=(vmem, vmem),
        scratch_shapes=[
            pltpu.VMEM((PAD, PAD, ROWS, NORB), jnp.float32),
            pltpu.VMEM((PAD, PAD, ROWS, NORB), jnp.float32),
            pltpu.VMEM((NORB, NORB), jnp.float32),
        ],
        compiler_params=pltpu.CompilerParams(vmem_limit_bytes=40 * 1024 * 1024),
    )(orb_index.reshape(1), own, other, v)

    rho_all = lax.all_gather(rho, "frag", axis=0)
    places = offsets[assignment]
    signs = weight_signs[assignment].astype(jnp.float32) / NORB
    half = (slot_index - places[:, 0] // SLAB) % frag_count
    lands = half[:, None] == jnp.arange(2)[None, :]
    variant = (places[:, 1] // SLAB) * 3 + places[:, 2] // SLAB
    weights = jnp.where(
        lands[None] & (variant[None, :, None] == jnp.arange(6)[:, None, None]), signs[None, :, None], 0.0
    )
    summed = jnp.dot(
        weights.reshape(6, 2 * frag_count),
        rho_all.reshape(2 * frag_count, SLAB * PLANE),
        precision=HIGHEST,
        preferred_element_type=jnp.float32,
    ).reshape(6, SLAB, FSIDE, FSIDE)
    density = jnp.zeros((SLAB, GX, GY), jnp.float32)
    for i in range(6):
        ox, oy = 8 * (i // 3), 8 * (i % 3)
        density = density + jnp.pad(summed[i], ((0, 0), (ox, GX - FSIDE - ox), (oy, GY - FSIDE - oy)))
    return (density.reshape(SLAB, GX * GY), states[None])


def solution(mesh):
    return jax.shard_map(
        local,
        mesh=mesh,
        in_specs=(
            P(("parts", "frag"), None),
            P(("parts", "frag"), None, "orb"),
            P("parts", None),
            P("parts"),
            P("parts"),
        ),
        out_specs=(P(("parts", "frag"), None), P(("parts", "frag"), None, "orb")),
        check_vma=False,
    )
```

time: 463 us -> 166 us (0.36); the launches traced: 455 us -> 166 us
  waiting for transfers between devices: 158 us -> 0.01 us
  starting transfers between devices: 109 us -> 0.52 us
  other arithmetic: 96.5 us -> 2.01 us
  Pallas kernels: 0 us -> 86.2 us
  blocking collectives: 37 us -> 62.8 us
  matrix products: 17.9 us -> 0.25 us
  between operations: 25 us -> 8.82 us
  local copies, waits for them, and re-layouts: 10.8 us -> 5.57 us
    ppermute x50 -> x1, starting transfers between devices: 109 us -> 0.52 us  [local(): other = lax.ppermute(own.astype(jnp.float32), 'orb', [(0, 1), (1, 0)])]
    pallas_call x0 -> x1, Pallas kernels: none -> 86.2 us  [local(): pl.pallas_call(fragment_kernel, out_shape=(jax.ShapeDtypeStruct((NORB, SL...]
    psum x4 -> x0, waiting for transfers between devices: 74.2 us -> none  [summed_gram(): return lax.psum(gram(left, right), 'orb')]
    another operation x15 -> x0, other arithmetic: 68.6 us -> none  [the longest x9 37.2 us: orthonormal(): lower = jnp.linalg.cholesky(matrix)]
    reduce_scatter x1 -> x0, waiting for transfers between devices: 61.5 us -> none  [local(): lax.psum_scatter(jnp.dot(pick, placed, precision=lax.Precision.HIGHEST, p...]
    all_gather x0 -> x1, blocking collectives: none -> 30.5 us  [local(): rho_all = lax.all_gather(rho, 'frag', axis=0)]
    ppermute x50 -> x1, waiting for transfers between devices: 22.3 us -> 0.01 us  [local(): other = lax.ppermute(own.astype(jnp.float32), 'orb', [(0, 1), (1, 0)])]
    sub x22 -> x0, other arithmetic: 21.1 us -> none  [the longest x21 20.3 us: chebyshev(): 2.0 * (operate(current) - SPECTRUM_MID * current) / SPECTRUM_HALF - previous]
  transfers between devices with their start and end apart: 55 -> 1, of which waited for: 29 -> 0; matrix products, arithmetic and copies ran while one was open for 1% -> 3% of each run, Pallas kernels for 0% -> 0%
where the time goes in v1:
time: 166 us
  Pallas kernels  86.2 us (52%)
  blocking collectives  62.8 us (38%)
  between operations  8.82 us (5%)
  local copies, waits for them, and re-layouts  5.57 us (3%)
  other arithmetic  2.01 us (1%)
    pallas_call x1, Pallas kernels, local(): pl.pallas_call(fragment_kernel, out_shape=(jax.ShapeDtypeStruct((NORB, SL...  86.2 us
    all_gather x1, blocking collectives, local(): piece = lax.all_gather(potential, 'frag', axis=0, tiled=True)  32.3 us
    all_gather x1, blocking collectives, local(): rho_all = lax.all_gather(rho, 'frag', axis=0)  30.5 us
  transfers between devices with their start and end apart: 1, of which 0 were waited for; matrix products, arithmetic and copies ran while one was open for 3% of the time, Pallas kernels for 0%

profile of v1, /device:TPU:0, one launch (start us, length us, event | category | flops | bytes accessed | tf_op | source)
XLA Modules:
  0.0 166.1 jit_solution(521951976978945960)
XLA Ops:
  0.6 0.0 copy-start
  0.7 1.2 bitcast_convert_fusion
  1.8 0.5 collective-permute-start
  2.3 1.2 dynamic_slice.9
  4.9 32.3 %all_gather.9 = f32[64,768]{1,0:T(8,128)S(1)} all-gather(f32[8,768]{1,0:T(8,128)} %param.5), channel_id=1, replica_groups=mesh['parts'=2,'frag'=8,'orb'=2] {'frag'}, dimensions={0}, use_global_device_ids=true | all-gather | bytes 221184 | tf_op jit(solution)/shard_map/all_gather | solution.py:183
  37.2 0.2 copy.12
  38.0 0.1 constant_dynamic-slice_fusion
  38.1 0.6 fusion.6
  42.7 0.2 copy.13
  42.8 0.6 gather_fusion.1
  45.6 0.2 pad_maximum_fusion
  45.7 0.1 add_multiply_fusion
  45.8 0.1 copy.11
  45.9 0.1 copy.14
  46.0 0.6 gather_fusion
  46.6 0.2 fusion.3
  46.8 0.1 iota_compare_fusion
  46.9 0.1 iota_compare_fusion.1
  47.0 0.1 and_select_fusion
  47.1 0.6 broadcast_in_dim.34.v_ref
  47.7 86.2 %shard_map.68 = (f32[128,2048]{1,0:T(8,128)}, f32[16,256]{1,0:T(8,128)S(1)}) custom-call(s32[1]{0:T(128)} %bitcast.1.orb_ref, bf16[128,2048]{1,0:T(8,128)(2,1)S(1)} %bitcast.12, f32[128,2048]{1,0:T(8,128)S(1)} %collective-permute-done.other_ref, f32[16,16,16,128]{3,2,1,0:T(8,128)S(1)} %broadcast_in_dim.34.v_ref), custom_call_target="tpu_custom_call" | custom-call | tf_op jit(solution)/shard_map/pallas_call | solution.py:189
  133.8 30.5 %all-gather = f32[128,256]{1,0:T(8,128)S(1)} all-gather(f32[16,256]{1,0:T(8,128)S(1)} %get-tuple-element.4), channel_id=2, replica_groups=mesh['parts'=2,'frag'=8,'orb'=2] {'frag'}, dimensions={0}, use_global_device_ids=true | all-gather | bytes 147456 | tf_op jit(solution)/shard_map/all_gather | solution.py:205
  164.4 0.3 fusion.7
  164.6 0.1 slice_reduce_fusion.5
  164.8 0.1 squeeze.48
  164.9 0.1 squeeze.49
  164.9 0.1 squeeze.50
  165.0 0.1 squeeze.51
  165.1 0.1 squeeze.52
  165.2 0.1 squeeze.53
  165.3 0.1 pad_add_fusion
  165.4 0.7 reshape.202
  (14 shorter events, 0.1 us)
Async XLA Ops:
  0.6 42.2 %copy-start = (s32[8]{0:T(128)S(1)}, s32[8]{0:T(128)}, u32[]{:S(2)}) copy-start(s32[8]{0:T(128)} %param.8) | copy-start | bytes 100
  0.6 36.7 %copy-start.3 = (s32[8]{0:T(128)S(1)}, s32[8]{0:T(128)}, u32[]{:S(2)}) copy-start(s32[8]{0:T(128)} %param.9) | copy-start | bytes 100
  0.7 37.3 %copy-start.2 = (s32[8,3]{0,1:T(4,128)S(1)}, s32[8,3]{0,1:T(4,128)}, u32[]{:S(2)}) copy-start(s32[8,3]{0,1:T(4,128)} %param.7) | copy-start | bytes 292
  1.8 45.2 %collective-permute-start = (f32[128,2048]{1,0:T(8,128)S(1)}, f32[128,2048]{1,0:T(8,128)S(1)}, u32[]{:S(2)}, u32[]{:S(2)}) collective-permute-start(f32[128,2048]{1,0:T(8,128)S(1)} %bitcast_convert_fusion), channel_id=1, source_target_pairs={{0,1},{1,0},{2,3},{3,2},{4,5},{5,4},{6,7},{7,6},{8,9},{9,8},{10,11... | collective-permute-start | bytes 3145736 | tf_op jit(solution)/shard_map/ppermute | solution.py:180
  43.5 4.2 %copy-start.1 = (bf16[1,128,2048]{2,1,0:T(8,128)(2,1)S(1)}, bf16[1,128,2048]{2,1,0:T(8,128)(2,1)}, u32[]{:S(2)}) copy-start(bf16[1,128,2048]{2,1,0:T(8,128)(2,1)} %param.6) | copy-start | bytes 1572868

commit v2 on v1

--- a/solution.py
+++ b/solution.py
@@ -1,3 +1,5 @@
+import functools
+
 import jax
 import jax.numpy as jnp
 from jax import lax
@@ -67,8 +69,21 @@
     return jnp.concatenate(out, axis=0)
 
 
-def fragment_kernel(orb_ref, own_ref, other_ref, v_ref, states_ref, rho_ref, xa, xb, w_ref):
-    orb = orb_ref[0]
+def fragment_kernel(
+    offsets_ref, assign_ref, own_ref, other_ref, pot_ref, states_ref, rho_ref, xa, xb, v_ref, turned, w_ref
+):
+    orb = lax.axis_index("orb")
+    frag_count = pot_ref.shape[0]
+    f = assign_ref[lax.axis_index("frag")]
+    oz, ox, oy = offsets_ref[f, 0], offsets_ref[f, 1], offsets_ref[f, 2]
+    for half in range(2):
+        slab = pot_ref[lax.rem(oz // SLAB + half, frag_count)]
+        turned[half] = ((slab + (3.0 - SPECTRUM_MID)) * (2.0 / SPECTRUM_HALF)).T
+    for half in range(2):
+        for x in range(FSIDE):
+            cells = turned[half, pl.ds(pl.multiple_of((ox + x) * GY + oy, 8), FSIDE), :]
+            for z in range(SLAB):
+                v_ref[half * SLAB + z, x] = jnp.broadcast_to(cells[:, z : z + 1], (FSIDE, NORB))
 
     def clear(z, _):
         xa[z] = jnp.zeros((PAD, ROWS, NORB), jnp.float32)
@@ -172,56 +187,144 @@
         states_ref[:, PLANE * z : PLANE * (z + 1)] = plane(xa, orb * SLAB + z).T
 
 
+def peer(**where):
+    return {"device_id": where, "device_id_type": pl.DeviceIdType.MESH}
+
+
+def greet(frag_count, with_orb):
+    me, orb = lax.axis_index("frag"), lax.axis_index("orb")
+    barrier = pltpu.get_barrier_semaphore()
+
+    def hello(i, c):
+        pl.semaphore_signal(barrier, inc=1, **peer(frag=lax.rem(me + i, frag_count)))
+        return c
+
+    lax.fori_loop(1, frag_count, hello, 0)
+    if with_orb:
+        pl.semaphore_signal(barrier, inc=1, **peer(orb=1 - orb))
+    pl.semaphore_wait(barrier, frag_count - 1 + int(with_orb))
+
+
+def spread(frag_count, source, gathered, send_sem, recv_sem):
+    me = lax.axis_index("frag")
+
+    def copy_to(i):
+        return pltpu.make_async_remote_copy(
+            src_ref=source,
+            dst_ref=gathered.at[me],
+            send_sem=send_sem.at[i - 1],
+            recv_sem=recv_sem.at[i - 1],
+            **peer(frag=lax.rem(me + i, frag_count)),
+        )
+
+    def start(i, c):
+        copy_to(i).start()
+        return c
+
+    def wait(i, c):
+        copy_to(i).wait()
+        return c
+
+    lax.fori_loop(1, frag_count, start, 0)
+    return lambda: lax.fori_loop(1, frag_count, wait, 0)
+
+
+def gather_kernel(frag_count, pot_ref, own_ref, all_ref, other_ref, wide, send_sem, recv_sem, orb_sems):
+    greet(frag_count, True)
+    finish = spread(frag_count, pot_ref, all_ref, send_sem, recv_sem)
+    wide[...] = own_ref[...].astype(jnp.float32)
+    swap = pltpu.make_async_remote_copy(
+        src_ref=wide, dst_ref=other_ref, send_sem=orb_sems.at[0], recv_sem=orb_sems.at[1],
+        **peer(orb=1 - lax.axis_index("orb")),
+    )
+    swap.start()
+    all_ref[lax.axis_index("frag")] = pot_ref[...]
+    finish()
+    swap.wait()
+
+
+def patch_kernel(frag_count, offsets_ref, signs_ref, assign_ref, rho_ref, out_ref, all_ref, send_sem, recv_sem):
+    me = lax.axis_index("frag")
+    greet(frag_count, False)
+    finish = spread(frag_count, rho_ref, all_ref, send_sem, recv_sem)
+    all_ref[me] = rho_ref[...]
+    rows = lax.broadcasted_iota(jnp.int32, (PLANE, 2 * PLANE), 0)
+    columns = lax.broadcasted_iota(jnp.int32, (PLANE, 2 * PLANE), 1)
+    widen = (columns == 2 * rows - rows % FSIDE).astype(jnp.float32)
+    finish()
+
+    def add(d, sums):
+        f = assign_ref[d]
+        oz, ox, oy = offsets_ref[f, 0], offsets_ref[f, 1], offsets_ref[f, 2]
+        half = lax.rem(me - oz // SLAB + frag_count, frag_count)
+        sign = signs_ref[f].astype(jnp.float32) / NORB
+        value = all_ref[d]
+        lower = value[:SLAB] * jnp.where(half == 0, sign, 0.0)
+        upper = value[SLAB:] * jnp.where(half == 1, sign, 0.0)
+        both = lower + upper
+        return tuple(
+            sums[i] + both * jnp.where((ox == 8 * (i // 3)) & (oy == 8 * (i % 3)), 1.0, 0.0)
+            for i in range(6)
+        )
+
+    sums = lax.fori_loop(0, frag_count, add, (jnp.zeros((SLAB, PLANE), jnp.float32),) * 6)
+    wide = dot(jnp.concatenate(sums, axis=0), widen, ((1,), (0,)))
+    out_ref[...] = jnp.zeros_like(out_ref)
+    for i in range(6):
+        part = wide[SLAB * i : SLAB * (i + 1)]
+        if i % 3:
+            part = pltpu.roll(part, 8 * (i % 3), 1)
+        start = PLANE * (i // 3)
+        out_ref[:, start : start + 2 * PLANE] += part
+
+
 def local(potential, orbitals, offsets, weight_signs, assignment):
     frag_count = lax.axis_size("frag")
-    slot_index = lax.axis_index("frag")
-    orb_index = lax.axis_index("orb")
     own = orbitals[0]
-    other = lax.ppermute(own.astype(jnp.float32), "orb", [(0, 1), (1, 0)])
-    place = offsets[assignment[slot_index]]
-    zero_idx = place[0] * 0
-    piece = lax.all_gather(potential, "frag", axis=0, tiled=True)
-    piece = jnp.concatenate([piece, piece[:SLAB]], axis=0).reshape(-1, GX, GY)
-    v = lax.dynamic_slice(piece, (place[0], place[1], place[2]), (FSIDE, FSIDE, FSIDE))
-    v = (v + (3.0 - SPECTRUM_MID)) * (2.0 / SPECTRUM_HALF)
-    v = jnp.broadcast_to(v[..., None], (FSIDE, FSIDE, FSIDE, NORB))
     vmem = pl.BlockSpec(memory_space=pltpu.VMEM)
+    smem = pl.BlockSpec(memory_space=pltpu.SMEM)
+    sems = pltpu.SemaphoreType.DMA((frag_count - 1,))
+    all_pot, other = pl.pallas_call(
+        functools.partial(gather_kernel, frag_count),
+        out_shape=(
+            jax.ShapeDtypeStruct((frag_count,) + potential.shape, jnp.float32),
+            jax.ShapeDtypeStruct(own.shape, jnp.float32),
+        ),
+        in_specs=[vmem, vmem],
+        out_specs=(vmem, vmem),
+        scratch_shapes=[pltpu.VMEM(own.shape, jnp.float32), sems, sems, pltpu.SemaphoreType.DMA((2,))],
+        compiler_params=pltpu.CompilerParams(
+            collective_id=0, has_side_effects=True, vmem_limit_bytes=24 * 1024 * 1024
+        ),
+    )(potential, own)
     states, rho = pl.pallas_call(
         fragment_kernel,
         out_shape=(
             jax.ShapeDtypeStruct((NORB, SLAB * PLANE), jnp.float32),
             jax.ShapeDtypeStruct((FSIDE, PLANE), jnp.float32),
         ),
-        in_specs=[pl.BlockSpec(memory_space=pltpu.SMEM), vmem, vmem, vmem],
+        in_specs=[smem, smem, vmem, vmem, vmem],
         out_specs=(vmem, vmem),
         scratch_shapes=[
             pltpu.VMEM((PAD, PAD, ROWS, NORB), jnp.float32),
             pltpu.VMEM((PAD, PAD, ROWS, NORB), jnp.float32),
+            pltpu.VMEM((FSIDE, FSIDE, FSIDE, NORB), jnp.float32),
+            pltpu.VMEM((2, GX * GY, SLAB), jnp.float32),
             pltpu.VMEM((NORB, NORB), jnp.float32),
         ],
         compiler_params=pltpu.CompilerParams(vmem_limit_bytes=40 * 1024 * 1024),
-    )(orb_index.reshape(1), own, other, v)
-
-    rho_all = lax.all_gather(rho, "frag", axis=0)
-    places = offsets[assignment]
-    signs = weight_signs[assignment].astype(jnp.float32) / NORB
-    half = (slot_index - places[:, 0] // SLAB) % frag_count
-    lands = half[:, None] == jnp.arange(2)[None, :]
-    variant = (places[:, 1] // SLAB) * 3 + places[:, 2] // SLAB
-    weights = jnp.where(
-        lands[None] & (variant[None, :, None] == jnp.arange(6)[:, None, None]), signs[None, :, None], 0.0
-    )
-    summed = jnp.dot(
-        weights.reshape(6, 2 * frag_count),
-        rho_all.reshape(2 * frag_count, SLAB * PLANE),
-        precision=HIGHEST,
-        preferred_element_type=jnp.float32,
-    ).reshape(6, SLAB, FSIDE, FSIDE)
-    density = jnp.zeros((SLAB, GX, GY), jnp.float32)
-    for i in range(6):
-        ox, oy = 8 * (i // 3), 8 * (i % 3)
-        density = density + jnp.pad(summed[i], ((0, 0), (ox, GX - FSIDE - ox), (oy, GY - FSIDE - oy)))
-    return (density.reshape(SLAB, GX * GY), states[None])
+    )(offsets, assignment, own, other, all_pot)
+    density = pl.pallas_call(
+        functools.partial(patch_kernel, frag_count),
+        out_shape=jax.ShapeDtypeStruct((SLAB, GX * GY), jnp.float32),
+        in_specs=[smem, smem, smem, vmem],
+        out_specs=vmem,
+        scratch_shapes=[pltpu.VMEM((frag_count, FSIDE, PLANE), jnp.float32), sems, sems],
+        compiler_params=pltpu.CompilerParams(
+            collective_id=1, has_side_effects=True, vmem_limit_bytes=24 * 1024 * 1024
+        ),
+    )(offsets, weight_signs, assignment, rho)
+    return (density, states[None])
 
 
 def solution(mesh):

time: 166 us -> 111 us (0.67)
  blocking collectives: 62.8 us -> 0 us
  Pallas kernels: 86.2 us -> 106 us
  between operations: 8.82 us -> 0.67 us
  other arithmetic: 2.01 us -> 0 us
    all_gather x2 -> x0, blocking collectives: 62.8 us -> none  [the longest x1 32.3 us: local(): piece = lax.all_gather(potential, 'frag', axis=0, tiled=True)]
    pallas_call x0 -> x2, Pallas kernels: none -> 19.2 us  [the longest x1 10.2 us: local(): pl.pallas_call(functools.partial(gather_kernel, frag_count), out_shape=(j...]
    unnamed x9 -> x12, local copies, waits for them, and re-layouts: 0.11 us -> 4.44 us
  transfers between devices with their start and end apart: 1 -> 0, of which waited for: 0 -> 0; matrix products, arithmetic and copies ran while one was open for 3% -> 0% of each run, Pallas kernels for 0% -> 0%
where the time goes in v2:
time: 111 us
  Pallas kernels  106 us (95%)
  local copies, waits for them, and re-layouts  4.44 us (4%)
    pallas_call x1, Pallas kernels, local(): pl.pallas_call(fragment_kernel, out_shape=(jax.ShapeDtypeStruct((NORB, SL...  86.9 us
    pallas_call x1, Pallas kernels, local(): pl.pallas_call(functools.partial(gather_kernel, frag_count), out_shape=(j...  10.2 us
    pallas_call x1, Pallas kernels, local(): pl.pallas_call(functools.partial(patch_kernel, frag_count), out_shape=jax...  8.93 us
    unnamed x12, local copies, waits for them, and re-layouts  4.44 us

profile of v2, /device:TPU:0, one launch (start us, length us, event | category | flops | bytes accessed | tf_op | source)
XLA Modules:
  0.0 111.2 jit_solution(2621873933779678898)
XLA Ops:
  0.6 0.8 copy.8.offsets_ref
  1.4 0.0 copy-start
  1.4 1.0 copy-done
  2.4 0.0 copy-start.2
  2.4 0.7 copy-done.2
  3.2 0.0 copy-start.1
  3.2 10.2 %shard_map.68 = (f32[8,8,768]{2,1,0:T(8,128)S(1)}, f32[128,2048]{1,0:T(8,128)S(1)}) custom-call(f32[8,768]{1,0:T(8,128)S(1)} %copy-done.2, bf16[128,2048]{1,0:T(8,128)(2,1)S(1)} %bitcast.2), custom_call_target="tpu_custom_call" | custom-call | tf_op jit(solution)/shard_map/pallas_call | solution.py:287
  13.4 0.0 copy-start.3
  13.4 0.0 copy-done.1
  13.4 0.6 copy-done.3
  14.1 86.9 %shard_map.69 = (f32[128,2048]{1,0:T(8,128)}, f32[16,256]{1,0:T(8,128)S(1)}) custom-call(s32[8,3]{1,0:T(8,128)S(1)} %copy.8.offsets_ref, s32[8]{0:T(128)S(1)} %copy-done.3, bf16[128,2048]{1,0:T(8,128)(2,1)S(1)} %bitcast.3, f32[128,2048]{1,0:T(8,128)S(1)} %get-tuple-element.6.other_ref, f32[8,8,768]{2,1,0:T(8,128)S(1)} %get-tuple-element.7.pot_ref), custom_call_target="tpu_custom_call" | custom-call | tf_op jit(solution)/shard_map/pallas_call | solution.py:300
  101.0 0.0 copy-start.4
  101.0 0.7 copy-done.4
  101.7 8.9 %shard_map.70 = f32[8,768]{1,0:T(8,128)S(1)} custom-call(s32[8,3]{1,0:T(8,128)S(1)} %copy.8.offsets_ref, s32[8]{0:T(128)S(1)} %copy-done.4, s32[8]{0:T(128)S(1)} %copy-done.3, f32[16,256]{1,0:T(8,128)S(1)} %get-tuple-element.8.rho_ref), custom_call_target="tpu_custom_call" | custom-call | tf_op jit(solution)/shard_map/pallas_call | solution.py:317
  110.6 0.6 copy.10
Async XLA Ops:
  1.4 1.0 copy-start
  2.4 0.7 copy-start.2
  3.2 10.3 %copy-start.1 = (bf16[1,128,2048]{2,1,0:T(8,128)(2,1)S(1)}, bf16[1,128,2048]{2,1,0:T(8,128)(2,1)}, u32[]{:S(2)}) copy-start(bf16[1,128,2048]{2,1,0:T(8,128)(2,1)} %param.6) | copy-start | bytes 1572868
  13.4 0.7 copy-start.3
  101.0 0.7 copy-start.4

commit v3 on v2

--- a/solution.py
+++ b/solution.py
@@ -19,6 +19,7 @@
 PAD = FSIDE + 2
 ROWS = 32
 LOW = 8
+UNROLL = 4
 
 SPECTRUM_MID = 3.5
 SPECTRUM_HALF = 3.75
@@ -31,6 +32,25 @@
     return lax.dot_general(
         left, right, (dims, ((), ())), precision=HIGHEST, preferred_element_type=jnp.float32
     )
+
+
+def pieces(x):
+    high = x.astype(jnp.bfloat16)
+    return jnp.concatenate([high, (x - high.astype(jnp.float32)).astype(jnp.bfloat16)], axis=1)
+
+
+def packed_dot(left, right, dims):
+    return lax.dot_general(left, right, (dims, ((), ())), preferred_element_type=jnp.float32)
+
+
+def quadrants(x):
+    x = x[:NORB] + x[NORB:]
+    return x[:, :NORB] + x[:, NORB:]
+
+
+def twice(x):
+    both = pieces(x)
+    return jnp.concatenate([both, both], axis=0)
 
 
 def inverse_factor(matrix):
@@ -100,28 +120,45 @@
 
     mid = pl.ds(LOW, FSIDE)
 
-    def stencil(src, z, x):
-        c = src[z + 1, x + 1, mid, :]
-        n = src[z, x + 1, mid, :] + src[z + 2, x + 1, mid, :]
-        n = n + (src[z + 1, x, mid, :] + src[z + 1, x + 2, mid, :])
-        n = n + (src[z + 1, x + 1, pl.ds(LOW - 1, FSIDE), :] + src[z + 1, x + 1, pl.ds(LOW + 1, FSIDE), :])
-        return v_ref[z, x] * c - COUPLE * n
+    def sweep(src, planes, z0, emit):
+        held = {}
+
+        def at(k, x):
+            if (k, x) not in held:
+                held[k, x] = src[z0 + k, x, mid, :]
+            return held[k, x]
+
+        for x in range(FSIDE):
+            for k in range(planes):
+                c = at(k + 1, x + 1)
+                n = at(k, x + 1) + at(k + 2, x + 1)
+                n = n + (at(k + 1, x) + at(k + 1, x + 2))
+                n = n + (
+                    src[z0 + k + 1, x + 1, pl.ds(LOW - 1, FSIDE), :]
+                    + src[z0 + k + 1, x + 1, pl.ds(LOW + 1, FSIDE), :]
+                )
+                emit(k, x, v_ref[z0 + k, x] * c - COUPLE * n, c)
 
     def first(src, dst):
-        def body(z, _):
-            for x in range(FSIDE):
-                dst[z + 1, x + 1, mid, :] = 0.5 * stencil(src, z, x)
+        def body(i, _):
+            def emit(k, x, value, c):
+                dst[UNROLL * i + k + 1, x + 1, mid, :] = 0.5 * value
+
+            sweep(src, UNROLL, UNROLL * i, emit)
             return 0
 
-        lax.fori_loop(0, FSIDE, body, 0)
+        lax.fori_loop(0, FSIDE // UNROLL, body, 0)
 
     def later(src, dst):
-        def body(z, _):
-            for x in range(FSIDE):
-                dst[z + 1, x + 1, mid, :] = stencil(src, z, x) - dst[z + 1, x + 1, mid, :]
+        def body(i, _):
+            def emit(k, x, value, c):
+                z = UNROLL * i + k + 1
+                dst[z, x + 1, mid, :] = value - dst[z, x + 1, mid, :]
+
+            sweep(src, UNROLL, UNROLL * i, emit)
             return 0
 
-        lax.fori_loop(0, FSIDE, body, 0)
+        lax.fori_loop(0, FSIDE // UNROLL, body, 0)
 
     def plane(src, z):
         return src[z + 1, 1 : FSIDE + 1, mid, :].reshape(PLANE, NORB)
@@ -138,30 +175,33 @@
         lax.fori_loop(0, DEGREE // 2 - 1, pair, 0)
 
         def add(z, total):
-            y = plane(xa, z)
-            return total + dot(y, y, ((0,), (0,)))
-
-        total = lax.fori_loop(0, FSIDE, add, jnp.zeros((NORB, NORB), jnp.float32))
-        w_ref[...] = inverse_factor(total / FCELLS)
+            y = pieces(plane(xa, z))
+            return total + packed_dot(y, y, ((0,), (0,)))
+
+        total = lax.fori_loop(0, FSIDE, add, jnp.zeros((2 * NORB, 2 * NORB), jnp.float32), unroll=2)
+        w_ref[...] = twice(inverse_factor(quadrants(total) / FCELLS).T)
 
         def apply(z, c):
-            s = dot(plane(xa, z), w_ref[...], ((1,), (1,)))
+            s = packed_dot(pieces(plane(xa, z)), w_ref[...], ((1,), (0,)))
+            s = s[:, :NORB] + s[:, NORB:]
             xa[z + 1, 1 : FSIDE + 1, mid, :] = s.reshape(FSIDE, FSIDE, NORB)
             return c
 
-        lax.fori_loop(0, FSIDE, apply, 0)
+        lax.fori_loop(0, FSIDE, apply, 0, unroll=2)
         return carry
 
     lax.fori_loop(0, PASSES, one_pass, 0)
 
     def couple(z, total):
         parts = []
-        for x in range(FSIDE):
-            parts.append((SPECTRUM_HALF / 2) * stencil(xa, z, x) + SPECTRUM_MID * xa[z + 1, x + 1, mid, :])
+        sweep(
+            xa, 1, z, lambda k, x, value, c: parts.append((SPECTRUM_HALF / 2) * value + SPECTRUM_MID * c)
+        )
         h = jnp.concatenate(parts, axis=0)
-        return total + dot(plane(xa, z), h, ((0,), (0,)))
-
-    coupling = lax.fori_loop(0, FSIDE, couple, jnp.zeros((NORB, NORB), jnp.float32)) / FCELLS
+        return total + packed_dot(pieces(plane(xa, z)), pieces(h), ((0,), (0,)))
+
+    total = lax.fori_loop(0, FSIDE, couple, jnp.zeros((2 * NORB, 2 * NORB), jnp.float32))
+    coupling = quadrants(total) / FCELLS
     projected = 0.5 * (coupling + coupling.T)
     rows = lax.broadcasted_iota(jnp.int32, (NORB, NORB), 0)
     columns = lax.broadcasted_iota(jnp.int32, (NORB, NORB), 1)
@@ -172,17 +212,18 @@
         square = dot(occupied, occupied, ((1,), (0,)))
         cube = dot(square, occupied, ((1,), (0,)))
         occupied = 3.0 * square - 2.0 * cube
-    w_ref[...] = occupied
-    ones = jnp.ones((8, NORB), jnp.float32)
+    w_ref[...] = twice(occupied)
+    ones = jnp.ones((8, 2 * NORB), jnp.bfloat16)
 
     def density(z, c):
         s = plane(xa, z)
-        m = s * dot(s, w_ref[...], ((1,), (0,)))
-        r = dot(ones, m, ((1,), (1,)))
+        m = packed_dot(pieces(s), w_ref[...], ((1,), (0,)))
+        m = s * (m[:, :NORB] + m[:, NORB:])
+        r = packed_dot(ones, pieces(m), ((1,), (1,)))
         rho_ref[pl.ds(z, 1), :] = r[0:1]
         return c
 
-    lax.fori_loop(0, FSIDE, density, 0)
+    lax.fori_loop(0, FSIDE, density, 0, unroll=2)
     for z in range(SLAB):
         states_ref[:, PLANE * z : PLANE * (z + 1)] = plane(xa, orb * SLAB + z).T
 
@@ -310,7 +351,7 @@
             pltpu.VMEM((PAD, PAD, ROWS, NORB), jnp.float32),
             pltpu.VMEM((FSIDE, FSIDE, FSIDE, NORB), jnp.float32),
             pltpu.VMEM((2, GX * GY, SLAB), jnp.float32),
-            pltpu.VMEM((NORB, NORB), jnp.float32),
+            pltpu.VMEM((2 * NORB, 2 * NORB), jnp.bfloat16),
         ],
         compiler_params=pltpu.CompilerParams(vmem_limit_bytes=40 * 1024 * 1024),
     )(offsets, assignment, own, other, all_pot)

time: 111 us -> 79.9 us (0.72)
  Pallas kernels: 106 us -> 74.5 us
    pallas_call x1, Pallas kernels: 86.9 us -> 55.3 us  [local(): pl.pallas_call(fragment_kernel, out_shape=(jax.ShapeDtypeStruct((NORB, SL...]
where the time goes in v3:
time: 79.9 us; the launch traced here: 79.6 us
  Pallas kernels  74.5 us (93%)
  local copies, waits for them, and re-layouts  4.44 us (6%)
    pallas_call x1, Pallas kernels, local(): pl.pallas_call(fragment_kernel, out_shape=(jax.ShapeDtypeStruct((NORB, SL...  55.3 us
    pallas_call x1, Pallas kernels, local(): pl.pallas_call(functools.partial(gather_kernel, frag_count), out_shape=(j...  10.2 us
    pallas_call x1, Pallas kernels, local(): pl.pallas_call(functools.partial(patch_kernel, frag_count), out_shape=jax...  8.93 us
    unnamed x12, local copies, waits for them, and re-layouts  4.44 us

profile of v3, /device:TPU:0, one launch (start us, length us, event | category | flops | bytes accessed | tf_op | source)
XLA Modules:
  0.0 79.6 jit_solution(14283681631346948008)
XLA Ops:
  0.6 0.8 copy.8.offsets_ref
  1.4 0.0 copy-start
  1.4 1.0 %copy-done = bf16[1,128,2048]{2,1,0:T(8,128)(2,1)S(1)} copy-done((bf16[1,128,2048]{2,1,0:T(8,128)(2,1)S(1)}, bf16[1,128,2048]{2,1,0:T(8,128)(2,1)}, u32[]{:S(2)}) %copy-start) | copy-done | bytes 524312
  2.4 0.0 copy-start.2
  2.4 0.7 copy-done.2
  3.2 0.0 copy-start.1
  3.2 10.2 %shard_map.68 = (f32[8,8,768]{2,1,0:T(8,128)S(1)}, f32[128,2048]{1,0:T(8,128)S(1)}) custom-call(f32[8,768]{1,0:T(8,128)S(1)} %copy-done.2, bf16[128,2048]{1,0:T(8,128)(2,1)S(1)} %bitcast.2), custom_call_target="tpu_custom_call" | custom-call | tf_op jit(solution)/shard_map/pallas_call | solution.py:328
  13.4 0.0 copy-start.3
  13.4 0.0 copy-done.1
  13.4 0.6 copy-done.3
  14.1 55.3 %shard_map.69 = (f32[128,2048]{1,0:T(8,128)}, f32[16,256]{1,0:T(8,128)S(1)}) custom-call(s32[8,3]{1,0:T(8,128)S(1)} %copy.8.offsets_ref, s32[8]{0:T(128)S(1)} %copy-done.3, bf16[128,2048]{1,0:T(8,128)(2,1)S(1)} %bitcast.3, f32[128,2048]{1,0:T(8,128)S(1)} %get-tuple-element.6.other_ref, f32[8,8,768]{2,1,0:T(8,128)S(1)} %get-tuple-element.7.pot_ref), custom_call_target="tpu_custom_call" | custom-call | tf_op jit(solution)/shard_map/pallas_call | solution.py:341
  69.4 0.0 copy-start.4
  69.4 0.7 copy-done.4
  70.1 8.9 %shard_map.70 = f32[8,768]{1,0:T(8,128)S(1)} custom-call(s32[8,3]{1,0:T(8,128)S(1)} %copy.8.offsets_ref, s32[8]{0:T(128)S(1)} %copy-done.4, s32[8]{0:T(128)S(1)} %copy-done.3, f32[16,256]{1,0:T(8,128)S(1)} %get-tuple-element.8.rho_ref), custom_call_target="tpu_custom_call" | custom-call | tf_op jit(solution)/shard_map/pallas_call | solution.py:358
  79.0 0.6 copy.10
Async XLA Ops:
  1.4 1.0 %copy-start = (bf16[1,128,2048]{2,1,0:T(8,128)(2,1)S(1)}, bf16[1,128,2048]{2,1,0:T(8,128)(2,1)}, u32[]{:S(2)}) copy-start(bf16[1,128,2048]{2,1,0:T(8,128)(2,1)} %param.6) | copy-start | bytes 1572868
  2.4 0.7 copy-start.2
  3.2 10.3 %copy-start.1 = (bf16[1,128,2048]{2,1,0:T(8,128)(2,1)S(1)}, bf16[1,128,2048]{2,1,0:T(8,128)(2,1)}, u32[]{:S(2)}) copy-start(bf16[1,128,2048]{2,1,0:T(8,128)(2,1)} %param.6) | copy-start | bytes 1572868
  13.4 0.7 copy-start.3
  69.4 0.7 copy-start.4

commit v4 on v3

--- a/solution.py
+++ b/solution.py
@@ -20,6 +20,7 @@
 ROWS = 32
 LOW = 8
 UNROLL = 4
+CHUNKS = 4
 
 SPECTRUM_MID = 3.5
 SPECTRUM_HALF = 3.75
@@ -105,12 +106,19 @@
             for z in range(SLAB):
                 v_ref[half * SLAB + z, x] = jnp.broadcast_to(cells[:, z : z + 1], (FSIDE, NORB))
 
+    for ref in (xa, xb):
+        for z in (0, PAD - 1):
+            ref[z] = jnp.zeros((PAD, ROWS, NORB), jnp.float32)
+
     def clear(z, _):
-        xa[z] = jnp.zeros((PAD, ROWS, NORB), jnp.float32)
-        xb[z] = jnp.zeros((PAD, ROWS, NORB), jnp.float32)
+        for ref in (xa, xb):
+            for x in (0, PAD - 1):
+                ref[z, x] = jnp.zeros((ROWS, NORB), jnp.float32)
+            ref[z, :, 0:LOW, :] = jnp.zeros((PAD, LOW, NORB), jnp.float32)
+            ref[z, :, LOW + FSIDE : ROWS, :] = jnp.zeros((PAD, LOW, NORB), jnp.float32)
         return 0
 
-    lax.fori_loop(0, PAD, clear, 0)
+    lax.fori_loop(1, PAD - 1, clear, 0)
 
     for z in range(SLAB):
         block = own_ref[:, PLANE * z : PLANE * (z + 1)].astype(jnp.float32).T
@@ -178,7 +186,7 @@
             y = pieces(plane(xa, z))
             return total + packed_dot(y, y, ((0,), (0,)))
 
-        total = lax.fori_loop(0, FSIDE, add, jnp.zeros((2 * NORB, 2 * NORB), jnp.float32), unroll=2)
+        total = lax.fori_loop(0, FSIDE, add, jnp.zeros((2 * NORB, 2 * NORB), jnp.float32), unroll=4)
         w_ref[...] = twice(inverse_factor(quadrants(total) / FCELLS).T)
 
         def apply(z, c):
@@ -187,7 +195,7 @@
             xa[z + 1, 1 : FSIDE + 1, mid, :] = s.reshape(FSIDE, FSIDE, NORB)
             return c
 
-        lax.fori_loop(0, FSIDE, apply, 0, unroll=2)
+        lax.fori_loop(0, FSIDE, apply, 0, unroll=4)
         return carry
 
     lax.fori_loop(0, PASSES, one_pass, 0)
@@ -223,7 +231,7 @@
         rho_ref[pl.ds(z, 1), :] = r[0:1]
         return c
 
-    lax.fori_loop(0, FSIDE, density, 0, unroll=2)
+    lax.fori_loop(0, FSIDE, density, 0, unroll=4)
     for z in range(SLAB):
         states_ref[:, PLANE * z : PLANE * (z + 1)] = plane(xa, orb * SLAB + z).T
 
@@ -273,15 +281,22 @@
 def gather_kernel(frag_count, pot_ref, own_ref, all_ref, other_ref, wide, send_sem, recv_sem, orb_sems):
     greet(frag_count, True)
     finish = spread(frag_count, pot_ref, all_ref, send_sem, recv_sem)
-    wide[...] = own_ref[...].astype(jnp.float32)
-    swap = pltpu.make_async_remote_copy(
-        src_ref=wide, dst_ref=other_ref, send_sem=orb_sems.at[0], recv_sem=orb_sems.at[1],
-        **peer(orb=1 - lax.axis_index("orb")),
-    )
-    swap.start()
+    other = 1 - lax.axis_index("orb")
+    swaps = []
+    for i in range(CHUNKS):
+        part = pl.ds(i * (NORB // CHUNKS), NORB // CHUNKS)
+        wide[part, :] = own_ref[part, :].astype(jnp.float32)
+        swaps.append(
+            pltpu.make_async_remote_copy(
+                src_ref=wide.at[part, :], dst_ref=other_ref.at[part, :],
+                send_sem=orb_sems.at[0, i], recv_sem=orb_sems.at[1, i], **peer(orb=other),
+            )
+        )
+        swaps[-1].start()
     all_ref[lax.axis_index("frag")] = pot_ref[...]
     finish()
-    swap.wait()
+    for swap in swaps:
+        swap.wait()
 
 
 def patch_kernel(frag_count, offsets_ref, signs_ref, assign_ref, rho_ref, out_ref, all_ref, send_sem, recv_sem):
@@ -291,7 +306,7 @@
     all_ref[me] = rho_ref[...]
     rows = lax.broadcasted_iota(jnp.int32, (PLANE, 2 * PLANE), 0)
     columns = lax.broadcasted_iota(jnp.int32, (PLANE, 2 * PLANE), 1)
-    widen = (columns == 2 * rows - rows % FSIDE).astype(jnp.float32)
+    widen = jnp.where(columns == 2 * rows - rows % FSIDE, 1.0, 0.0).astype(jnp.bfloat16)
     finish()
 
     def add(d, sums):
@@ -309,7 +324,10 @@
         )
 
     sums = lax.fori_loop(0, frag_count, add, (jnp.zeros((SLAB, PLANE), jnp.float32),) * 6)
-    wide = dot(jnp.concatenate(sums, axis=0), widen, ((1,), (0,)))
+    sums = jnp.concatenate(sums, axis=0)
+    high = sums.astype(jnp.bfloat16)
+    rest = (sums - high.astype(jnp.float32)).astype(jnp.bfloat16)
+    wide = packed_dot(high, widen, ((1,), (0,))) + packed_dot(rest, widen, ((1,), (0,)))
     out_ref[...] = jnp.zeros_like(out_ref)
     for i in range(6):
         part = wide[SLAB * i : SLAB * (i + 1)]
@@ -333,7 +351,7 @@
         ),
         in_specs=[vmem, vmem],
         out_specs=(vmem, vmem),
-        scratch_shapes=[pltpu.VMEM(own.shape, jnp.float32), sems, sems, pltpu.SemaphoreType.DMA((2,))],
+        scratch_shapes=[pltpu.VMEM(own.shape, jnp.float32), sems, sems, pltpu.SemaphoreType.DMA((2, CHUNKS))],
         compiler_params=pltpu.CompilerParams(
             collective_id=0, has_side_effects=True, vmem_limit_bytes=24 * 1024 * 1024
         ),

time: 79.9 us -> 74.4 us (0.931)
  Pallas kernels: 74.5 us -> 69.1 us
    pallas_call x1, Pallas kernels: 55.3 us -> 50 us  [local(): pl.pallas_call(fragment_kernel, out_shape=(jax.ShapeDtypeStruct((NORB, SL...]
where the time goes in v4:
time: 74.4 us; the launch traced here: 74.2 us
  Pallas kernels  69.1 us (93%)
  local copies, waits for them, and re-layouts  4.44 us (6%)
    pallas_call x1, Pallas kernels, local(): pl.pallas_call(fragment_kernel, out_shape=(jax.ShapeDtypeStruct((NORB, SL...  50 us
    pallas_call x1, Pallas kernels, local(): pl.pallas_call(functools.partial(gather_kernel, frag_count), out_shape=(j...  10.3 us
    pallas_call x1, Pallas kernels, local(): pl.pallas_call(functools.partial(patch_kernel, frag_count), out_shape=jax...  8.71 us
    unnamed x12, local copies, waits for them, and re-layouts  4.44 us

profile of v4, /device:TPU:0, one launch (start us, length us, event | category | flops | bytes accessed | tf_op | source)
XLA Modules:
  0.0 74.2 jit_solution(14037258200178464520)
XLA Ops:
  0.6 0.8 %copy.8.offsets_ref = s32[8,3]{1,0:T(8,128)S(1)} copy(s32[8,3]{0,1:T(4,128)} %param.7) | data formatting | bytes 192 | tf_op args[2]
  1.4 0.0 copy-start
  1.4 1.0 %copy-done = bf16[1,128,2048]{2,1,0:T(8,128)(2,1)S(1)} copy-done((bf16[1,128,2048]{2,1,0:T(8,128)(2,1)S(1)}, bf16[1,128,2048]{2,1,0:T(8,128)(2,1)}, u32[]{:S(2)}) %copy-start) | copy-done | bytes 524312
  2.4 0.0 copy-start.2
  2.4 0.7 copy-done.2
  3.2 0.0 copy-start.1
  3.2 10.3 %shard_map.68 = (f32[8,8,768]{2,1,0:T(8,128)S(1)}, f32[128,2048]{1,0:T(8,128)S(1)}) custom-call(f32[8,768]{1,0:T(8,128)S(1)} %copy-done.2, bf16[128,2048]{1,0:T(8,128)(2,1)S(1)} %bitcast.2), custom_call_target="tpu_custom_call" | custom-call | tf_op jit(solution)/shard_map/pallas_call | solution.py:346
  13.5 0.0 copy-start.3
  13.5 0.0 copy-done.1
  13.5 0.6 copy-done.3
  14.1 50.0 %shard_map.69 = (f32[128,2048]{1,0:T(8,128)}, f32[16,256]{1,0:T(8,128)S(1)}) custom-call(s32[8,3]{1,0:T(8,128)S(1)} %copy.8.offsets_ref, s32[8]{0:T(128)S(1)} %copy-done.3, bf16[128,2048]{1,0:T(8,128)(2,1)S(1)} %bitcast.3, f32[128,2048]{1,0:T(8,128)S(1)} %get-tuple-element.6.other_ref, f32[8,8,768]{2,1,0:T(8,128)S(1)} %get-tuple-element.7.pot_ref), custom_call_target="tpu_custom_call" | custom-call | tf_op jit(solution)/shard_map/pallas_call | solution.py:359
  64.2 0.0 copy-start.4
  64.2 0.7 copy-done.4
  64.8 8.7 %shard_map.70 = f32[8,768]{1,0:T(8,128)S(1)} custom-call(s32[8,3]{1,0:T(8,128)S(1)} %copy.8.offsets_ref, s32[8]{0:T(128)S(1)} %copy-done.4, s32[8]{0:T(128)S(1)} %copy-done.3, f32[16,256]{1,0:T(8,128)S(1)} %get-tuple-element.8.rho_ref), custom_call_target="tpu_custom_call" | custom-call | tf_op jit(solution)/shard_map/pallas_call | solution.py:376
  73.6 0.6 copy.10
Async XLA Ops:
  1.4 1.0 %copy-start = (bf16[1,128,2048]{2,1,0:T(8,128)(2,1)S(1)}, bf16[1,128,2048]{2,1,0:T(8,128)(2,1)}, u32[]{:S(2)}) copy-start(bf16[1,128,2048]{2,1,0:T(8,128)(2,1)} %param.6) | copy-start | bytes 1572868
  2.4 0.7 copy-start.2
  3.2 10.3 %copy-start.1 = (bf16[1,128,2048]{2,1,0:T(8,128)(2,1)S(1)}, bf16[1,128,2048]{2,1,0:T(8,128)(2,1)}, u32[]{:S(2)}) copy-start(bf16[1,128,2048]{2,1,0:T(8,128)(2,1)} %param.6) | copy-start | bytes 1572868
  13.5 0.7 copy-start.3
  64.2 0.7 copy-start.4
